TPU v7x, 256 devices: a whole 4x4x8 slice. The times are simulated.
256 devices in a mesh: lon: 16 (over z, core), lat: 16 (over x, y).
Axes of the slice: x: 4, y: 4, z: 8, core: 2. Of those that a mesh axis runs over, the one named last changes fastest.
Arguments:
- innovation: float32 [16384], P(('lon', 'lat')), may hold values from -6 to 6
- ray_id: int32 [16, 16, 64], P('lon', 'lat'), may hold values from 0 to 16383
- cell_index: int32 [16, 16, 64, 128], P('lon', 'lat'), may hold values from 0 to 131071
- seg_length: float32 [16, 16, 64, 128], P('lon', 'lat'), may hold values from 0.2 to 2
- vertical_modes: float32 [128, 128], replicated, may hold values from -2 to 2
- lon_decay: float32 [128, 512], replicated, as said below
- lat_decay: float32 [128, 512], replicated, as said below
Outputs:
- increment: float32 [512, 512, 128], P('lon', 'lat')
Inputs may be any that keep to these rules, and one draw needn't show every extreme that they name: ray_id holds global observation indices. cell_index holds tile-local cell indices. `lon_decay`: every entry lies strictly between 0 and 1. `lat_decay`: every entry lies strictly between 0 and 1.
All inputs are finite; a program needn't handle non-finite values.
Results may differ from a plain program's by a relative error of at most 0.00018.
Values sent between devices are 32-bit elements; how exact they have to be, the bound alone decides.
A program may use at most 64 MiB of HBM per device.

v0:
```python
import jax
import jax.numpy as jnp
from jax import lax
from jax.sharding import PartitionSpec as P

L = 128
M = 128
CL = 32
CT = 32


def entering_2(value, axis, join, neutral, backward):
    count, mine = (lax.axis_size(axis), lax.axis_index(axis))
    pieces = jax.tree.map(lambda part: lax.all_gather(part, axis), value)
    if backward:
        pieces = jax.tree.map(lambda part: part[::-1], pieces)
        mine = count - 1 - mine
    total = jax.tree.map(
        lambda part, zero: jnp.full_like(part, 0) + jnp.asarray(zero, part.dtype), value, neutral
    )

    def hop(position, total):
        longer = join(total, jax.tree.map(lambda part: part[position], pieces))
        return jax.tree.map(lambda new, old: jnp.where(position < mine, new, old), longer, total)

    return lax.fori_loop(0, count - 1, hop, total)


def block_solve(local_logs, inputs):
    cells = local_logs.shape[0]
    cumulative = jnp.cumsum(local_logs, 0)
    lower = jnp.arange(cells)[:, None] >= jnp.arange(cells)[None, :]
    log_gaps = jnp.where(lower[:, :, None], cumulative[:, None, :] - cumulative[None, :, :], 0.0)
    kernel = jnp.where(lower[:, :, None], jnp.exp(log_gaps), 0.0)
    opened = jnp.einsum("rqm,qwm->rwm", kernel, inputs, precision=lax.Precision.HIGHEST)
    return (opened, jnp.exp(cumulative))


def chain(earlier, later):
    return (earlier[0] * later[0], jnp.expand_dims(later[0], -2) * earlier[1] + later[1])


def prepare(grid_field, decay_table, offset, reverse):
    span_cells = grid_field.shape[0]
    chain_len = decay_table.shape[1]
    log_decay = jnp.log(decay_table).T
    amplitude = lax.dynamic_slice_in_dim((1.0 - decay_table.T) ** 0.75, offset, span_cells, 0)
    places = jnp.arange(chain_len)
    if reverse:
        log_decay = jnp.roll(log_decay, -1, 0)
        local_logs = lax.dynamic_slice_in_dim(log_decay, offset, span_cells, 0)[::-1]
        inputs = grid_field[::-1]
        beyond = places < offset
    else:
        local_logs = lax.dynamic_slice_in_dim(log_decay, offset, span_cells, 0)
        inputs = amplitude[:, None, :] * grid_field
        beyond = places >= offset + span_cells
    return (log_decay, local_logs, inputs, amplitude, beyond)


def finish(states, amplitude, reverse):
    if reverse:
        return amplitude[:, None, :] * states[::-1]
    return states


def lat_carry(grid_field, decay_table, reverse):
    turned = jnp.swapaxes(grid_field, 0, 1)
    offset = lax.axis_index("lat") * turned.shape[0]
    log_decay, local_logs, inputs, amplitude, beyond = prepare(turned, decay_table, offset, reverse)
    opened, growth = block_solve(local_logs, inputs)
    summary = (growth[-1], opened[-1])
    identity = (jnp.ones_like(growth[-1]), jnp.zeros_like(opened[-1]))
    entering_map = entering_2(summary, "lat", chain, identity, reverse)
    states = opened + growth[:, None, :] * entering_map[1][None]
    return jnp.swapaxes(finish(states, amplitude, reverse), 0, 1)


def periodic_rows(inputs, log_decay, blocks):
    span_cells = inputs.shape[0] // blocks
    pieces = inputs.reshape(blocks, span_cells, inputs.shape[1], inputs.shape[2])
    log_pieces = log_decay.reshape(blocks, span_cells, log_decay.shape[1])
    opened, growth = lax.map(
        lambda element: block_solve(element[0], element[1]), (log_pieces, pieces)
    )
    inclusive = lax.associative_scan(chain, (growth[:, -1], opened[:, -1]))
    total_growth = inclusive[0][-1]
    start_state = inclusive[1][-1] / (1.0 - total_growth)[None, :]
    end_states = inclusive[0][:, None, :] * start_state[None] + inclusive[1]
    entering = jnp.roll(end_states, 1, 0)
    states = opened + growth[:, :, None, :] * entering[:, None]
    return states.reshape(inputs.shape)


def lon_rows(grid_field, decay_table):
    lon_parts = lax.axis_size("lon")
    row_field = lax.all_to_all(grid_field, "lon", split_axis=1, concat_axis=0, tiled=True)
    log_decay = jnp.log(decay_table).T
    amplitude = (1.0 - decay_table.T) ** 0.75
    back_logs = jnp.roll(log_decay, -1, 0)[::-1]
    row_field = amplitude[:, None, :] * periodic_rows(row_field[::-1], back_logs, lon_parts)[::-1]
    row_field = periodic_rows(amplitude[:, None, :] * row_field, log_decay, lon_parts)
    return lax.all_to_all(row_field, "lon", split_axis=0, concat_axis=1, tiled=True)


def on_device(innovation, ray_id, cell_index, seg_length, vertical_modes, lon_decay, lat_decay):
    all_innovations = lax.all_gather(innovation, ("lon", "lat"), axis=0, tiled=True)
    values = seg_length[0, 0] * jnp.take(all_innovations, ray_id[0, 0])[:, None]
    forcing = jax.ops.segment_sum(
        values.reshape(-1), cell_index[0, 0].reshape(-1), num_segments=CL * CT * L
    )
    mode_field = jnp.dot(
        forcing.reshape(CL * CT, L), vertical_modes, precision=lax.Precision.HIGHEST
    )
    mode_field = mode_field.reshape(CL, CT, M)
    mode_field = lat_carry(lat_carry(mode_field, lat_decay, True), lat_decay, False)
    mode_field = lon_rows(mode_field, lon_decay)
    result = jnp.dot(
        mode_field.reshape(CL * CT, M), vertical_modes.T, precision=lax.Precision.HIGHEST
    )
    return result.reshape(CL, CT, L)


def solution(mesh):
    placed = (
        P(("lon", "lat")),
        P("lon", "lat", None),
        P("lon", "lat", None, None),
        P("lon", "lat", None, None),
        P(),
        P(),
        P(),
    )
    return jax.shard_map(
        on_device, mesh=mesh, in_specs=placed, out_specs=P("lon", "lat", None), check_vma=False
    )
```

profile of v0, /device:TPU:1, one launch (start us, length us, event | category | flops | bytes accessed | tf_op | source)
XLA Modules:
  0.0 585.5 jit_solution(12302151993562260593)
XLA Ops:
  11.2 17.1 %all-gather = f32[16,1,128]{2,1,0:T(1,128)S(1)} all-gather(f32[1,1,128]{2,1,0:T(1,128)S(1)} %slice_bitcast_fusion.4), channel_id=1, replica_groups=mesh['lon'=16,'lat'=16] {'lat'}, dimensions={0}, use_global_device_ids=true | all-gather | bytes 8704 | tf_op jit(solution)/shard_map/all_gather | solution.py:14
  28.3 16.0 %all-gather.1 = f32[16,1,128]{2,1,0:T(1,128)S(1)} all-gather(f32[1,1,128]{2,1,0:T(1,128)S(1)} %slice_bitcast_fusion.3), channel_id=1, replica_groups=mesh['lon'=16,'lat'=16] {'lat'}, dimensions={0}, use_global_device_ids=true | all-gather | bytes 8704 | tf_op jit(solution)/shard_map/all_gather | solution.py:14
  44.3 210.4 %all-reduce.35.cloned.1.call-done = f32[16384]{0:T(1024)} async-done(((f32[16384]{0:T(1024)}), f32[16384]{0:T(1024)}) %all-reduce.35.cloned.1.call-update) | async-done | bytes 65552
  256.4 43.5 %scatter_custom_fusion = f32[131072]{0:T(1024)S(1)} fusion(s32[8192]{0:T(1024)} %bitcast.191, f32[8192]{0:T(1024)S(1)} %bitcast_multiply_fusion, f32[]{:T(128)} %constant.104.clone.1), kind=kCustom, calls=%fused_computation.74 | custom fusion | flops 8192 | bytes 524800 | tf_op jit(solution)/shard_map/scatter-add | solution.py:109
  300.6 2.9 copy.103
  303.5 4.0 fusion.48
  307.7 17.4 %all_gather.17 = f32[16,32,128]{2,1,0:T(8,128)S(1)} all-gather(f32[1,32,128]{2,1,0:T(8,128)S(1)} %copy.105), channel_id=1, replica_groups=mesh['lon'=16,'lat'=16] {'lat'}, dimensions={0}, use_global_device_ids=true | all-gather | bytes 278528 | tf_op jit(solution)/shard_map/all_gather | solution.py:14
  327.8 2.4 rev.28
  330.2 2.8 fusion.36
  334.5 17.3 %all_gather.19 = f32[16,32,128]{2,1,0:T(8,128)S(1)} all-gather(f32[1,32,128]{2,1,0:T(8,128)S(1)} %copy.111), channel_id=1, replica_groups=mesh['lon'=16,'lat'=16] {'lat'}, dimensions={0}, use_global_device_ids=true | all-gather | bytes 278528 | tf_op jit(solution)/shard_map/all_gather | solution.py:14
  356.7 14.8 %all-to-all-start = ((f32[32,32,128]{2,0,1:T(8,128)}), f32[32,32,128]{2,0,1:T(8,128)S(1)}, u32[]{:S(2)}, u32[]{:S(2)}) async-start(f32[32,32,128]{2,0,1:T(8,128)} %copy.113), calls=%async_computation | async-start | bytes 1048576 | tf_op jit(solution)/shard_map/all_to_all | solution.py:97
  372.8 16.1 %all-to-all-done = f32[32,32,128]{2,0,1:T(8,128)S(1)} async-done(((f32[32,32,128]{2,0,1:T(8,128)}), f32[32,32,128]{2,0,1:T(8,128)S(1)}, u32[]{:S(2)}, u32[]{:S(2)}) %all-to-all-start) | async-done | bytes 524320 | tf_op jit(solution)/shard_map/all_to_all | solution.py:97
  388.9 2.6 rev.29
  392.3 76.3 %while.52 = (s32[]{:T(128)}, f32[16,32,2,128]{1,2,3,0:T(2,128)S(1)}, f32[16,32,128]{2,1,0:T(8,128)S(1)}, f32[16,32,2,128]{3,1,0,2:T(8,128)}, f32[16,32,128]{2,1,0:T(8,128)S(1)}, /*index=5*/s32[]{:T(128)}, f32[]{:T(128)}) while((s32[]{:T(128)}, f32[16,32,2,128]{1,2,3,0:T(2,128)S(1)}, f32[16,32,128]{2,1,0:T(8,128)S(1)}, ...), condition=%wide.region_9.10_spmd, body=%wide.region_7.9_spmd.sunk | while | flops 3666946 | bytes 660577 | solution.py:83
  393.4 3.7 fusion.99
  398.2 3.7 fusion.99
  402.9 3.7 fusion.99
  407.7 3.7 fusion.99
  412.5 3.7 fusion.99
  417.3 3.7 fusion.99
  422.0 3.7 fusion.99
  426.8 3.7 fusion.99
  431.6 3.7 fusion.99
  436.3 3.7 fusion.99
  441.1 3.7 fusion.99
  445.9 3.7 fusion.99
  450.7 3.7 fusion.99
  455.4 3.7 fusion.99
  460.2 3.7 fusion.99
  465.0 3.7 fusion.99
  476.2 76.3 %while.53 = (s32[]{:T(128)}, f32[16,32,2,128]{1,2,3,0:T(2,128)S(1)}, f32[16,32,128]{2,1,0:T(8,128)S(1)}, f32[16,32,2,128]{3,1,0,2:T(8,128)}, f32[16,32,128]{2,1,0:T(8,128)S(1)}, /*index=5*/s32[]{:T(128)}, f32[]{:T(128)}) while((s32[]{:T(128)}, f32[16,32,2,128]{1,2,3,0:T(2,128)S(1)}, f32[16,32,128]{2,1,0:T(8,128)S(1)}, ...), condition=%wide.region_12.13_spmd, body=%wide.region_10.12_spmd.sunk | while | flops 3666946 | bytes 660577 | solution.py:83
  477.3 3.7 fusion.102
  482.0 3.7 fusion.102
  486.8 3.7 fusion.102
  491.6 3.7 fusion.102
  496.4 3.7 fusion.102
  501.1 3.7 fusion.102
  505.9 3.7 fusion.102
  510.7 3.7 fusion.102
  515.4 3.7 fusion.102
  520.2 3.7 fusion.102
  525.0 3.7 fusion.102
  529.8 3.7 fusion.102
  534.5 3.7 fusion.102
  539.3 3.7 fusion.102
  544.1 3.7 fusion.102
  548.9 3.7 fusion.102
  556.7 20.1 %all_to_all.33 = f32[512,2,128]{2,1,0:T(2,128)S(1)} all-to-all(f32[512,2,128]{2,1,0:T(2,128)S(1)} %copy.126), channel_id=1, replica_groups=mesh['lon'=16,'lat'=16] {'lon'}, dimensions={0} | all-to-all | bytes 1048576 | tf_op jit(solution)/shard_map/all_to_all | solution.py:103
  (503 shorter events, 65.8 us)
Async XLA Ops:
  6.5 293.4 %copy-start = (f32[128,128]{1,0:T(8,128)S(1)}, f32[128,128]{1,0:T(8,128)}, u32[]{:S(2)}) copy-start(f32[128,128]{1,0:T(8,128)} %param.19) | copy-start | bytes 196612
  6.5 3.0 copy-start.5
  6.5 249.8 %copy-start.4 = (f32[1,1,64,128]{3,2,1,0:T(8,128)S(1)}, f32[1,1,64,128]{3,2,1,0:T(8,128)}, u32[]{:S(2)}) copy-start(f32[1,1,64,128]{3,2,1,0:T(8,128)} %param.18) | copy-start | bytes 98308
  6.5 248.2 %all-reduce.35.cloned.1.call-start = ((), (), s32[]{:S(2)}) async-start(), calls=%async_computation.2 | async-start | bytes 131072
  7.4 0.6 copy-start.3
  333.0 1.3 copy-start.1
  354.7 16.9 %copy-start.2 = (f32[128,512]{1,0:T(8,128)S(1)}, f32[128,512]{1,0:T(8,128)}, u32[]{:S(2)}) copy-start(f32[128,512]{1,0:T(8,128)} %param.20) | copy-start | bytes 786436
  356.7 32.1 %all-to-all-start = ((f32[32,32,128]{2,0,1:T(8,128)}), f32[32,32,128]{2,0,1:T(8,128)S(1)}, u32[]{:S(2)}, u32[]{:S(2)}) async-start(f32[32,32,128]{2,0,1:T(8,128)} %copy.113), calls=%async_computation | async-start | bytes 1048576 | tf_op jit(solution)/shard_map/all_to_all | solution.py:97
Sparse Core Ops, SparseCore 0:
  12.9 241.8 all-reduce.34
where the time goes:
time: 588 us; the launch traced here: 585 us
  waiting for transfers between devices  227 us (39%)
  matrix products  126 us (21%)
  blocking collectives  87.9 us (15%)
  local copies, waits for them, and re-layouts  60.9 us (10%)
  other arithmetic  52.6 us (9%)
  starting transfers between devices  14.8 us (3%)
  between operations  14.4 us (2%)
    unnamed x2, waiting for transfers between devices  210 us
    dot_general x34, matrix products, block_solve(): jnp.einsum('rqm,qwm->rwm', kernel, inputs, precision=lax.Precision.HIGHEST)  124 us
    all_gather x4, blocking collectives, entering_2(): pieces = jax.tree.map(lambda part: lax.all_gather(part, axis), value)  67.8 us
    scatter-add x1, other arithmetic, on_device(): jax.ops.segment_sum(values.reshape(-1), cell_index[0, 0].reshape(-1), num...  43.5 us
    dynamic_slice x64, local copies, waits for them, and re-layouts, periodic_rows(): lax.map(lambda element: block_solve(element[0], element[1]), (log_pieces,...  28.4 us
    all_to_all x1, blocking collectives, lon_rows(): lax.all_to_all(row_field, 'lon', split_axis=0, concat_axis=1, tiled=True)  20.1 us
    all_to_all x1, waiting for transfers between devices, lon_rows(): lax.all_to_all(grid_field, 'lon', split_axis=1, concat_axis=0, tiled=True)  16.1 us
    all_to_all x1, starting transfers between devices, lon_rows(): lax.all_to_all(grid_field, 'lon', split_axis=1, concat_axis=0, tiled=True)  14.8 us
  transfers between devices with their start and end apart: 2, of which 2 were waited for; matrix products, arithmetic and copies ran while one was open for 1% of the time, Pallas kernels for 0%

commit v1 on v0

v1 whole, which is shorter than its diff:
```python
import functools

import jax
import jax.numpy as jnp
from jax import lax
from jax.experimental import pallas as pl
from jax.experimental.pallas import tpu as pltpu
from jax.sharding import PartitionSpec as P

MESH = pl.DeviceIdType.MESH
BF = jnp.bfloat16
F32 = jnp.float32
CELLS = 32
TILES = 16
MODES = 128
ROWS = CELLS * CELLS
BLOCKS = 64
SAMP = 128
LAT_PEERS = (10, 2, 8, 9, 11, 6, 14, 5, 7, 13, 15, 1, 3, 4, 12)
LON_PEERS = (8, 9, 7, 6, 10, 5, 11, 4, 12, 3, 13, 2, 14, 1, 15)
CHIP_PEERS = (4, 3, 5, 2, 6, 1, 7)


def split(value):
    high = value.astype(BF)
    return high, (value - high.astype(F32)).astype(BF)


def one_hot_rows(cell_ref, cells_hot, start, stop):
    def body(block, _):
        cell = cell_ref[pl.ds(block, 1), :]
        lon = lax.shift_right_logical(cell, 12)
        lat = jnp.bitwise_and(lax.shift_right_logical(cell, 7), CELLS - 1)
        place = lax.broadcasted_iota(jnp.int32, (CELLS, SAMP), 0)
        lat_hot = (place == lat).astype(F32).astype(BF)
        lon_hot = (place == lon).astype(F32)
        for row in range(CELLS):
            chosen = jnp.broadcast_to(lon_hot[row : row + 1], (CELLS, SAMP)).astype(BF)
            cells_hot[block, row * CELLS : (row + 1) * CELLS] = lat_hot * chosen
        return 0

    lax.fori_loop(start, stop, body, 0)


def valued_levels(cell_ref, value_ref, block):
    level = jnp.bitwise_and(cell_ref[pl.ds(block, 1), :], MODES - 1)
    hit = lax.broadcasted_iota(jnp.int32, (MODES, SAMP), 0) == level
    value = value_ref[pl.ds(block, 1), :]
    high = value.astype(BF).astype(F32)
    low = value - high
    return jnp.concatenate(
        [jnp.where(hit, high, 0.0).astype(BF), jnp.where(hit, low, 0.0).astype(BF)], axis=0
    )


def scatter(cell_ref, value_ref, cells_hot, acc, step=16):
    acc[...] = jnp.zeros_like(acc)

    def body(chunk, _):
        total = None
        for inner in range(0, step, 2):
            block = chunk * step + inner
            levels = jnp.concatenate(
                [valued_levels(cell_ref, value_ref, block + k) for k in range(2)], axis=1
            )
            cells = jnp.concatenate([cells_hot[block], cells_hot[block + 1]], axis=1)
            part = lax.dot_general(
                cells, levels, (((1,), (1,)), ((), ())), preferred_element_type=F32
            )
            total = part if total is None else total + part
        acc[...] += total
        return 0

    lax.fori_loop(0, BLOCKS // step, body, 0)


def tile_sums(table):
    def body(cell, carried):
        grow, var, gap = carried
        decay = table[pl.ds(cell, TILES, stride=CELLS), :]
        less = 1.0 - decay
        return (
            grow * decay,
            decay * decay * var + less * jnp.sqrt(less),
            gap + grow * less,
        )

    zero = jnp.zeros((TILES, MODES), F32)
    return lax.fori_loop(0, CELLS, body, (zero + 1.0, zero, zero))


def own_tables(table, first, var, decay_ref, var_ref, enter_ref, leave_ref):
    decay_ref[...] = table[pl.ds(pl.multiple_of(first, CELLS), CELLS), :]
    grow = jnp.ones((1, MODES), F32)
    for cell in range(CELLS):
        decay = decay_ref[cell : cell + 1, :]
        less = 1.0 - decay
        var = decay * decay * var + less * jnp.sqrt(less)
        grow = grow * decay
        var_ref[cell : cell + 1, :] = var
        enter_ref[cell : cell + 1, :] = grow
    grow = jnp.ones((1, MODES), F32)
    for cell in reversed(range(CELLS)):
        leave_ref[cell : cell + 1, :] = grow * var_ref[cell : cell + 1, :]
        grow = grow * decay_ref[cell : cell + 1, :]


def kernel(
    innov_hbm, ray_hbm, cell_hbm, seg_hbm, modes_hbm, lon_hbm, lat_hbm, out_ref,
    innov_ref, ray_ref, cell_ref, seg_ref, modes_ref, lon_ref, lat_ref, in_sems,
    cells_hot, acc, field, value, innov_row, all_innov, g1_buf,
    lon_table, lat_table, lon_grow, lat_grow, chip_grow,
    lon_decay, lon_var, lon_enter, lon_leave, lat_decay, lat_var, lat_enter, lat_leave,
    lon_state, pair_buf, chip_buf, lon_carry, lat_state, lat_buf, lon_corner, lat_corner,
    smooth, lon_total, lat_total,
    g1_send, g1_recv, g2_send, g2_recv, t1_send, t1_recv, t2_send, t2_recv,
    b1_send, b1_recv, l2_send, l2_recv, pair_send, pair_recv,
):
    loads = [
        pltpu.make_async_copy(src, dst, in_sems.at[k])
        for k, (src, dst) in enumerate(
            (
                (innov_hbm, innov_ref),
                (lon_hbm, lon_ref),
                (lat_hbm, lat_ref),
                (cell_hbm, cell_ref),
                (ray_hbm, ray_ref),
                (seg_hbm, seg_ref),
                (modes_hbm, modes_ref),
            )
        )
    ]
    for load in loads:
        load.start()
    innov_in, lon_in, lat_in, *late_in = loads
    p, q = lax.axis_index("lon"), lax.axis_index("lat")
    z, core = p // 2, p % 2
    q_bits = [(q // 2**k) % 2 for k in range(4)]
    partner = p + 1 - 2 * core

    def lat_peer(mask):
        peer = q
        for k in range(4):
            if (mask >> k) & 1:
                peer = peer + (1 - 2 * q_bits[k]) * 2**k
        return peer

    def lat_slot(tile):
        slot = 0
        for k in range(4):
            bit = 1 - q_bits[k] if (tile >> k) & 1 else q_bits[k]
            slot = slot + bit * 2**k
        return slot

    def lon_peer(offset):
        return (p + offset) % TILES

    barrier = pltpu.get_barrier_semaphore()
    for offset in LON_PEERS:
        pl.semaphore_signal(
            barrier, inc=1, device_id={"lon": lon_peer(offset)}, device_id_type=MESH
        )
    for mask in LAT_PEERS:
        pl.semaphore_signal(
            barrier, inc=1, device_id={"lat": lat_peer(mask)}, device_id_type=MESH
        )

    sent = []

    def push(src, dst, send_sem, recv_sem, device):
        copy = pltpu.make_async_remote_copy(
            src_ref=src, dst_ref=dst, send_sem=send_sem, recv_sem=recv_sem,
            device_id=device, device_id_type=MESH,
        )
        copy.start()
        sent.append(copy)
        return copy

    innov_row[...] = jnp.zeros_like(innov_row)
    innov_in.wait()
    innov_row[0:1, 0:64] = innov_ref[...]
    row = jnp.broadcast_to(innov_row[0:1, :], (8, 128))
    both = row + pltpu.roll(row, 64, 1)
    sub = lax.broadcasted_iota(jnp.int32, (8, 128), 0)
    lane = lax.broadcasted_iota(jnp.int32, (8, 128), 1)
    mine = (sub == q // 2) & (lane // 64 == q % 2)
    g1_buf[0] = jnp.where(mine, both, 0.0)

    pl.semaphore_wait(barrier, 2 * (TILES - 1))
    g1 = [
        push(g1_buf.at[0], g1_buf.at[m], g1_send.at[m], g1_recv.at[m], {"lat": lat_peer(m)})
        for m in LAT_PEERS
    ]

    lon_in.wait()
    lat_in.wait()
    for part in range(4):
        span = slice(part * 128, (part + 1) * 128)
        lon_table[span, :] = lon_ref[:, span].T
        lat_table[span, :] = lat_ref[:, span].T
    grow, var, gap = tile_sums(lon_table)
    lon_grow[...] = grow
    loop, loop_gap, loop_var = grow[0:1], gap[0:1], var[0:1]
    for tile in range(1, TILES):
        own = slice(tile, tile + 1)
        loop_var = grow[own] * grow[own] * loop_var + var[own]
        loop_gap = loop_gap + loop * gap[own]
        loop = loop * grow[own]
    enter_var = loop_var / (loop_gap * (1.0 + loop))
    for tile in range(TILES - 1):
        own = slice(tile, tile + 1)
        enter_var = jnp.where(
            tile < p, grow[own] * grow[own] * enter_var + var[own], enter_var
        )
    own_tables(lon_table, p * CELLS, enter_var, lon_decay, lon_var, lon_enter, lon_leave)
    loop_scale = 1.0 / loop_gap
    for chip in range(TILES // 2):
        chip_grow[chip : chip + 1, :] = grow[2 * chip : 2 * chip + 1] * grow[2 * chip + 1 : 2 * chip + 2]

    grow, var, gap = tile_sums(lat_table)
    lat_grow[...] = grow
    enter_var = jnp.zeros((1, MODES), F32)
    for tile in range(TILES - 1):
        own = slice(tile, tile + 1)
        enter_var = jnp.where(
            tile < q, grow[own] * grow[own] * enter_var + var[own], enter_var
        )
    own_tables(lat_table, q * CELLS, enter_var, lat_decay, lat_var, lat_enter, lat_leave)

    for load in late_in:
        load.wait()
    one_hot_rows(cell_ref, cells_hot, 0, BLOCKS // 4)

    for copy in g1:
        copy.wait_recv()
    total = g1_buf[0]
    for slot in range(1, TILES):
        total = total + g1_buf[slot]
    all_innov[p] = total
    g2 = [
        push(all_innov.at[p], all_innov.at[p], g2_send.at[o], g2_recv.at[o], {"lon": lon_peer(o)})
        for o in LON_PEERS
    ]

    one_hot_rows(cell_ref, cells_hot, BLOCKS // 4, BLOCKS)
    ray = jnp.broadcast_to(ray_ref[...].astype(F32), (BLOCKS, BLOCKS))
    diagonal = lax.broadcasted_iota(jnp.int32, (BLOCKS, BLOCKS), 0) == lax.broadcasted_iota(
        jnp.int32, (BLOCKS, BLOCKS), 1
    )
    ray = jnp.sum(jnp.where(diagonal, ray, 0.0), axis=1, keepdims=True).astype(jnp.int32)
    ray = jnp.broadcast_to(ray, (BLOCKS, 128))
    place = lax.broadcasted_iota(jnp.int32, (BLOCKS, 128), 1)
    row_hot = (place == ray // 128).astype(F32).astype(BF)
    lane_hot = place == ray % 128

    for copy in g2:
        copy.wait_recv()
    table = all_innov[...].reshape(128, 128)
    picked = jnp.zeros((BLOCKS, 128), F32)
    for _ in range(3):
        high = table.astype(BF)
        picked = picked + jnp.dot(row_hot, high, preferred_element_type=F32)
        table = table - high.astype(F32)
    picked = jnp.sum(jnp.where(lane_hot, picked, 0.0), axis=1, keepdims=True)
    value[...] = seg_ref[...] * picked

    scatter(cell_ref, value, cells_hot, acc)

    modes_high, modes_low = split(modes_ref[...])
    both = jnp.concatenate([modes_high, modes_low], axis=1)
    to_modes = jnp.concatenate([both, both], axis=0)

    def to_spectral(chunk, _):
        own = pl.ds(pl.multiple_of(chunk * 256, 256), 256)
        forcing = acc[own, 0:128] + acc[own, 128:256]
        parts = jnp.concatenate(split(forcing), axis=1)
        result = jnp.dot(parts, to_modes, preferred_element_type=F32)
        field[own, :] = result[:, 0:128] + result[:, 128:256]
        return 0

    lax.fori_loop(0, ROWS // 256, to_spectral, 0)

    def lon_rows(cell):
        return pl.ds(cell * CELLS, CELLS) if isinstance(cell, int) else pl.ds(
            pl.multiple_of(cell * CELLS, CELLS), CELLS
        )

    state = jnp.zeros((CELLS, MODES), F32)
    for cell in range(CELLS):
        own = slice(cell, cell + 1)
        state = lon_decay[own] * state + lon_var[own] * field[lon_rows(cell), :]
        smooth[lon_rows(cell), :] = state
    lon_state[0] = state
    back = jnp.zeros((CELLS, MODES), F32)
    for cell in reversed(range(CELLS)):
        own = slice(cell, cell + 1)
        smooth[lon_rows(cell), :] = smooth[lon_rows(cell), :] + lon_var[own] * back
        back = lon_decay[own] * (back + field[lon_rows(cell), :])
    lon_state[1] = back

    def corners(state):
        return (
            jnp.sum(lat_leave[...] * state, axis=0, keepdims=True),
            jnp.sum(lat_enter[...] * state, axis=0, keepdims=True),
        )

    ff, fb = corners(lon_state[0])
    bf_, bb = corners(lon_state[1])
    lon_corner[0] = jnp.concatenate([ff, fb, bf_, bb, jnp.zeros((4, MODES), F32)], axis=0)
    t1 = [
        push(lon_corner.at[0], lon_corner.at[o], t1_send.at[o], t1_recv.at[o], {"lon": lon_peer(o)})
        for o in LON_PEERS
    ]
    l1 = push(lon_state.at[1 - core], pair_buf, pair_send.at[0], pair_recv.at[0], {"lon": partner})

    state = jnp.zeros((CELLS, MODES), F32)
    for cell in range(CELLS):
        own = slice(cell, cell + 1)
        rows = pl.ds(cell, CELLS, stride=CELLS)
        state = lat_decay[own] * state + lat_var[own] * smooth[rows, :]
        field[rows, :] = state
    lat_state[0] = state
    back = jnp.zeros((CELLS, MODES), F32)
    for cell in reversed(range(CELLS)):
        own = slice(cell, cell + 1)
        rows = pl.ds(cell, CELLS, stride=CELLS)
        field[rows, :] = field[rows, :] + lat_var[own] * back
        back = lat_decay[own] * (back + smooth[rows, :])
    lat_state[1] = back

    l1.wait_recv()
    chip_state = pair_buf[...] + lon_grow[pl.ds(partner, 1), :] * lon_state[core]
    chip_buf[0] = chip_state
    sign = 1 - 2 * core
    l2 = [
        push(
            chip_buf.at[0], chip_buf.at[o], l2_send.at[o], l2_recv.at[o],
            {"lon": 2 * ((z + sign * o + 8) % 8) + core},
        )
        for o in CHIP_PEERS
    ]
    b1 = []
    for m in LAT_PEERS:
        top = m.bit_length() - 1
        b1.append(
            push(
                lat_state.at[q_bits[top]], lat_buf.at[m], b1_send.at[m], b1_recv.at[m],
                {"lat": lat_peer(m)},
            )
        )
    lat_buf[0] = lat_state[0]

    for copy in t1:
        copy.wait_recv()
    ahead = lon_corner[0]
    behind = lon_corner[0]
    for o in reversed(range(1, TILES)):
        ahead = lon_grow[pl.ds((p + TILES - o) % TILES, 1), :] * ahead + lon_corner[o]
        behind = lon_grow[pl.ds((p + o) % TILES, 1), :] * behind + lon_corner[TILES - o]
    sub = lax.broadcasted_iota(jnp.int32, (8, MODES), 0)
    lat_corner[0] = jnp.where(sub < 2, ahead, behind) * loop_scale
    t2 = [
        push(lat_corner.at[0], lat_corner.at[m], t2_send.at[m], t2_recv.at[m], {"lat": lat_peer(m)})
        for m in LAT_PEERS
    ]

    for copy in l2:
        copy.wait_recv()
    carry = chip_buf[0]
    for o in reversed(range(1, 8)):
        carry = chip_grow[pl.ds((z - sign * o + 8) % 8, 1), :] * carry + chip_buf[o]
    carry = carry * loop_scale
    lon_carry[core] = carry
    pair_buf[...] = lon_grow[pl.ds(p, 1), :] * carry + lon_state[core]
    l3 = push(pair_buf, lon_carry.at[core], pair_send.at[1], pair_recv.at[1], {"lon": partner})

    for copy in b1:
        copy.wait_recv()
    ahead = jnp.zeros((CELLS, MODES), F32)
    behind = jnp.zeros((CELLS, MODES), F32)
    for tile in range(TILES - 1):
        got = lat_buf[lat_slot(tile)]
        ahead = jnp.where(tile < q, lat_grow[tile : tile + 1, :] * ahead + got, ahead)
    for tile in reversed(range(1, TILES)):
        got = lat_buf[lat_slot(tile)]
        behind = jnp.where(tile > q, lat_grow[tile : tile + 1, :] * behind + got, behind)

    l3.wait_recv()
    for way in range(2):
        state = jnp.zeros((1, MODES), F32)
        back = jnp.zeros((1, MODES), F32)
        for cell in range(CELLS):
            own = slice(cell, cell + 1)
            state = lat_decay[own] * state + lat_var[own] * lon_carry[way, own, :]
            lon_total[way, own, :] = state
        for cell in reversed(range(CELLS)):
            own = slice(cell, cell + 1)
            lon_total[way, own, :] = lon_total[way, own, :] + lat_var[own] * back
            back = lat_decay[own] * (back + lon_carry[way, own, :])

    for copy in t2:
        copy.wait_recv()
    corner_ahead = jnp.zeros((8, MODES), F32)
    corner_behind = jnp.zeros((8, MODES), F32)
    for tile in range(TILES - 1):
        got = lat_corner[lat_slot(tile)]
        corner_ahead = jnp.where(
            tile < q, lat_grow[tile : tile + 1, :] * corner_ahead + got, corner_ahead
        )
    for tile in reversed(range(1, TILES)):
        got = lat_corner[lat_slot(tile)]
        corner_behind = jnp.where(
            tile > q, lat_grow[tile : tile + 1, :] * corner_behind + got, corner_behind
        )
    lat_total[0] = ahead + lon_enter[...] * corner_ahead[0:1] + lon_leave[...] * corner_ahead[2:3]
    lat_total[1] = behind + lon_enter[...] * corner_behind[1:2] + lon_leave[...] * corner_behind[3:4]

    both = jnp.concatenate([modes_high, modes_low], axis=0)
    to_levels = jnp.concatenate([both, both], axis=1)
    per = 8

    def to_grid(chunk, _):
        pieces = []
        for inner in range(per):
            cell = chunk * per + inner
            own = pl.ds(cell, 1)
            pieces.append(
                field[lon_rows(cell), :]
                + lon_enter[own, :] * lon_total[0]
                + lon_leave[own, :] * lon_total[1]
                + lat_enter[...] * lat_total[0, own, :]
                + lat_leave[...] * lat_total[1, own, :]
            )
        whole = jnp.concatenate(pieces, axis=0)
        parts = jnp.concatenate(split(whole), axis=1)
        result = lax.dot_general(
            parts, to_levels, (((1,), (1,)), ((), ())), preferred_element_type=F32
        )
        own = pl.ds(pl.multiple_of(chunk * (per * CELLS), per * CELLS), per * CELLS)
        out_ref[own, :] = result[:, 0:128] + result[:, 128:256]
        return 0

    lax.fori_loop(0, CELLS // per, to_grid, 0)

    for copy in sent:
        copy.wait_send()


def on_device(innovation, ray_id, cell_index, seg_length, vertical_modes, lon_decay, lat_decay):
    vmem = pl.BlockSpec(memory_space=pltpu.VMEM)
    tile = lambda *shape: pltpu.VMEM(shape, F32)
    sems = lambda count: pltpu.SemaphoreType.DMA((count,))
    result = pl.pallas_call(
        kernel,
        out_shape=jax.ShapeDtypeStruct((ROWS, MODES), F32),
        in_specs=[pl.BlockSpec(memory_space=pltpu.HBM)] * 7,
        out_specs=vmem,
        scratch_shapes=[
            tile(1, 64),
            pltpu.VMEM((1, BLOCKS), jnp.int32),
            pltpu.VMEM((BLOCKS, SAMP), jnp.int32),
            tile(BLOCKS, SAMP),
            tile(MODES, MODES),
            tile(MODES, TILES * CELLS),
            tile(MODES, TILES * CELLS),
            pltpu.SemaphoreType.DMA((7,)),
            pltpu.VMEM((BLOCKS, ROWS, SAMP), BF),
            tile(ROWS, 256),
            tile(ROWS, MODES),
            tile(BLOCKS, SAMP),
            tile(8, 128),
            tile(TILES, 8, 128),
            tile(TILES, 8, 128),
            tile(TILES * CELLS, MODES),
            tile(TILES * CELLS, MODES),
            tile(TILES, MODES),
            tile(TILES, MODES),
            tile(TILES // 2, MODES),
        ]
        + [tile(CELLS, MODES)] * 8
        + [
            tile(2, CELLS, MODES),
            tile(CELLS, MODES),
            tile(8, CELLS, MODES),
            tile(2, CELLS, MODES),
            tile(2, CELLS, MODES),
            tile(TILES, CELLS, MODES),
            tile(TILES, 8, MODES),
            tile(TILES, 8, MODES),
            tile(ROWS, MODES),
            tile(2, CELLS, MODES),
            tile(2, CELLS, MODES),
        ]
        + [sems(TILES)] * 10
        + [sems(8)] * 2
        + [sems(2)] * 2,
        compiler_params=pltpu.CompilerParams(
            collective_id=0, has_side_effects=True, vmem_limit_bytes=63 * 2**20
        ),
        name="covariance",
    )(
        innovation.reshape(1, 64),
        ray_id.reshape(1, BLOCKS),
        cell_index.reshape(BLOCKS, SAMP),
        seg_length.reshape(BLOCKS, SAMP),
        vertical_modes,
        lon_decay,
        lat_decay,
    )
    return result.reshape(CELLS, CELLS, MODES)


def solution(mesh):
    placed = (
        P(("lon", "lat")),
        P("lon", "lat", None),
        P("lon", "lat", None, None),
        P("lon", "lat", None, None),
        P(),
        P(),
        P(),
    )
    return jax.shard_map(
        on_device, mesh=mesh, in_specs=placed, out_specs=P("lon", "lat", None), check_vma=False
    )
```

time: 588 us -> 41 us (0.07)
  waiting for transfers between devices: 227 us -> 0 us
  matrix products: 126 us -> 0 us
  blocking collectives: 87.9 us -> 0 us
  local copies, waits for them, and re-layouts: 60.9 us -> 1.87 us
  other arithmetic: 52.6 us -> 0 us
  Pallas kernels: 0 us -> 39 us
  starting transfers between devices: 14.8 us -> 0 us
  between operations: 14.4 us -> 0.01 us
    unnamed x2 -> x0, waiting for transfers between devices: 210 us -> none
    dot_general x36 -> x0, matrix products: 126 us -> none  [the longest x34 124 us: block_solve(): jnp.einsum('rqm,qwm->rwm', kernel, inputs, precision=lax.Precision.HIGHEST)]
    all_gather x4 -> x0, blocking collectives: 67.8 us -> none  [entering_2(): pieces = jax.tree.map(lambda part: lax.all_gather(part, axis), value)]
    scatter-add x1 -> x0, other arithmetic: 43.5 us -> none  [on_device(): jax.ops.segment_sum(values.reshape(-1), cell_index[0, 0].reshape(-1), num...]
    pallas_call x0 -> x1, Pallas kernels: none -> 39 us  [on_device(): pl.pallas_call(kernel, out_shape=jax.ShapeDtypeStruct((ROWS, MODES), F32)...]
    dynamic_slice x65 -> x0, local copies, waits for them, and re-layouts: 28.5 us -> none  [the longest x64 28.4 us: periodic_rows(): lax.map(lambda element: block_solve(element[0], element[1]), (log_pieces,...]
    all_to_all x1 -> x0, blocking collectives: 20.1 us -> none  [lon_rows(): lax.all_to_all(row_field, 'lon', split_axis=0, concat_axis=1, tiled=True)]
    all_to_all x1 -> x0, waiting for transfers between devices: 16.1 us -> none  [lon_rows(): lax.all_to_all(grid_field, 'lon', split_axis=1, concat_axis=0, tiled=True)]
  transfers between devices with their start and end apart: 2 -> 0, of which waited for: 2 -> 0; matrix products, arithmetic and copies ran while one was open for 1% -> 0% of each run, Pallas kernels for 0% -> 0%
where the time goes in v1:
time: 41 us; the launch traced here: 40.9 us
  Pallas kernels  39 us (95%)
  local copies, waits for them, and re-layouts  1.87 us (5%)
    pallas_call x1, Pallas kernels, on_device(): pl.pallas_call(kernel, out_shape=jax.ShapeDtypeStruct((ROWS, MODES), F32)...  39 us
    unnamed x1, local copies, waits for them, and re-layouts  1.87 us

profile of v1, /device:TPU:1, one launch (start us, length us, event | category | flops | bytes accessed | tf_op | source)
XLA Modules:
  0.0 40.9 jit_solution(17010072579721246553)
XLA Ops:
  0.0 39.0 %covariance.1 = f32[1024,128]{1,0:T(8,128)} custom-call(f32[1,64]{1,0:T(1,128)} %bitcast.8, s32[1,64]{1,0:T(1,128)} %bitcast.9, s32[64,128]{1,0:T(8,128)} %bitcast.6, f32[64,128]{1,0:T(8,128)} %bitcast.7, f32[128,128]{1,0:T(8,128)} %modes_hbm.1, f32[128,512]{1,0:T(8,128)} %lon_hbm.1, f32[128,512]{1,0:T(8,128)} %lat_hbm.1), custom_call_target="tpu_custom_call" | custom-call | tf_op jit(solution)/shard_map/covariance/pallas_call | solution.py:453
  39.0 1.9 %copy.9 = f32[32,32,128]{2,1,0:T(8,128)} copy(f32[32,32,128]{2,1,0:T(8,128)} %bitcast.5) | data formatting | bytes 1048576
